TPU v7x, 32 devices: a whole 2x2x4 slice. The times are simulated.
32 devices in a mesh: gy: 8 (over z, core), gx: 4 (over y, x).
Axes of the slice: x: 2, y: 2, z: 4, core: 2. Of those that a mesh axis runs over, the one named last changes fastest.
Arguments:
- images: bfloat16 [16, 448, 1344], P(None, 'gy', 'gx'), may hold values from -6 to 6
- position: bfloat16 [32, 32, 768], P('gy', 'gx'), may hold values from -4 to 4
- stem_w: bfloat16 [27, 32], replicated, may hold values from -1.25 to 1.25
- stem_b: float32 [32], replicated, may hold values from -0.5 to 0.5
- patch_w: bfloat16 [6272, 768], replicated, may hold values from -0.078125 to 0.078125
- norm_one: float32 [768], replicated, may hold values from 0.25 to 1.75
- qkv_w: bfloat16 [768, 2304], replicated, may hold values from -0.21875 to 0.21875
- q_gain: float32 [768], replicated, may hold values from 0.8 to 5, as said below
- k_gain: float32 [768], replicated, may hold values from 0.8 to 5, as said below
- out_w: bfloat16 [768, 768], replicated, may hold values from -0.21875 to 0.21875
- norm_two: float32 [768], replicated, may hold values from 0.25 to 1.75
- mlp_in: bfloat16 [768, 3072], replicated, may hold values from -0.21875 to 0.21875
- mlp_out: bfloat16 [3072, 768], replicated, may hold values from -0.109375 to 0.109375
- norm_last: float32 [768], replicated, may hold values from 0.25 to 1.75
- head_w: bfloat16 [768, 1024], replicated, may hold values from -0.21875 to 0.21875
- head_b: float32 [1024], replicated, may hold values from -5 to 5
- dataset_action: int32 [16], replicated, may hold values from 0 to 1023
- sampled: int32 [16, 10], replicated, may hold values from 0 to 1023
- targets: float32 [16], replicated, may hold values from -5 to 5
Outputs:
- q_values: float32 [16, 1024], replicated
- frame_loss: float32 [16], replicated
- loss: float32 [], replicated
Inputs may be any that keep to these rules, and one draw needn't show every extreme that they name: `q_gain`: gains of the query and key norms are positive. `k_gain`: gains of the query and key norms are positive. `sampled`: sampled actions of a frame may repeat.
All inputs are finite; a program needn't handle non-finite values.
Results may differ from a plain program's by a relative error of at most 0.00073.
Values may be sent and summed in bfloat16 or wider, within the bound.
A program may use at most 192 MiB of HBM per device.

v0:
```python
import functools

import jax
import jax.numpy as jnp
import numpy as np
from jax import lax
from jax.experimental import pallas as pl
from jax.experimental.pallas import tpu as pltpu
from jax.sharding import PartitionSpec as P

HEAD_DIM = 64
PATCH = 14
eps = 1e-06
penalty_weight = 1.0
F32 = jnp.float32
BF16 = jnp.bfloat16
MESH = pl.DeviceIdType.MESH
VMEM_LIMIT = 56 * 1024 * 1024


def vmem():
    return pl.BlockSpec(memory_space=pltpu.VMEM)


def gelu(x):
    u = x * (0.7978845608028654 + (0.7978845608028654 * 0.044715) * (x * x))
    half = 0.5 * x
    return half + half * jnp.tanh(u)


def layer_norm(values, gain):
    centre = values - jnp.mean(values, -1, keepdims=True)
    spread = jnp.mean(centre * centre, -1, keepdims=True)
    return centre * lax.rsqrt(spread + eps) * gain


def borders(images):
    tall = jnp.transpose(images, (1, 0, 2))
    for axis, dim, width in (("gy", 0, 1), ("gx", 2, 3)):
        ends = lax.axis_size(axis) - 1
        head = lax.slice_in_dim(tall, 0, width, axis=dim)
        tail = lax.slice_in_dim(tall, tall.shape[dim] - width, tall.shape[dim], axis=dim)
        before = lax.ppermute(tail, axis, [(i, i + 1) for i in range(ends)])
        after = lax.ppermute(head, axis, [(i + 1, i) for i in range(ends)])
        tall = jnp.concatenate([before, tall, after], axis=dim)
    return tall


def band(stem_w):
    channels = stem_w.shape[1]
    rows = np.arange(9 * (PATCH + 2))
    row_off, rest = rows // (3 * (PATCH + 2)), rows % (3 * (PATCH + 2))
    col_in, colour = rest // 3, rest % 3
    col_out = np.arange(PATCH * channels) // channels
    wide = jnp.tile(stem_w, (1, PATCH))
    picks = np.zeros((3, rows.size, 27), np.float32)
    for col_off in range(3):
        picks[col_off, rows, row_off * 9 + col_off * 3 + colour] = 1
    spread = jnp.dot(jnp.asarray(picks.reshape(-1, 27), BF16), wide, preferred_element_type=F32)
    spread = spread.reshape(3, rows.size, -1)
    total = 0.0
    for col_off in range(3):
        keep = col_in[:, None] == col_out[None, :] + col_off
        total = total + jnp.where(keep, spread[col_off], 0.0)
    return total.astype(BF16)


def embed_kernel(tall_ref, pos_ref, band_ref, bias_ref, pw_hbm, out_ref, stem, pw, acc, sem):
    rows, frames, _ = tall_ref.shape
    rows = rows - 2
    patch_rows, patch_cols, width = pos_ref.shape
    feats = band_ref.shape[1]
    span = 3 * (PATCH + 2)
    load = pltpu.make_async_copy(pw_hbm, pw, sem)
    load.start()
    for col in range(patch_cols):
        cut = tall_ref[:, :, 3 * PATCH * col : 3 * PATCH * col + span]
        taps = jnp.concatenate([cut[off : off + rows] for off in range(3)], axis=-1)
        for i in range(patch_rows):
            part = taps[i * PATCH : (i + 1) * PATCH].reshape(PATCH * frames, 3 * span)
            conv = jnp.dot(part, band_ref[...], preferred_element_type=F32)
            made = gelu(conv + bias_ref[...]).astype(BF16)
            stem[:, col, i] = made.reshape(PATCH, frames, feats)
    load.wait()
    count = patch_cols * patch_rows * frames
    acc[...] = jnp.zeros_like(acc)

    def step(p, carry):
        acc[...] += jnp.dot(
            stem[p].reshape(count, feats),
            pw[pl.ds(pl.multiple_of(p * feats, 64), feats), :],
            preferred_element_type=F32,
        )
        return carry

    lax.fori_loop(0, PATCH, step, 0)
    pieces = []
    for col in range(patch_cols):
        for i in range(patch_rows):
            at = (col * patch_rows + i) * frames
            place = pos_ref[i, col : col + 1, :].astype(F32)
            pieces.append((acc[at : at + frames, :] + place).astype(BF16))
    made = jnp.concatenate(pieces, axis=0)
    tiles = patch_cols * patch_rows
    to = lax.broadcasted_iota(jnp.int32, (count, count), 0)
    fro = lax.broadcasted_iota(jnp.int32, (count, count), 1)
    swap = jnp.where((to % tiles) * frames + to // tiles == fro, 1.0, 0.0).astype(BF16)
    out_ref[...] = (
        jnp.dot(swap, made, preferred_element_type=F32).astype(BF16).reshape(frames, tiles, width)
    )


def embed(tall, position, stem_w, stem_b, patch_w):
    patch_rows, patch_cols, width = position.shape
    frames = tall.shape[1]
    feats = PATCH * stem_w.shape[1]
    count = patch_rows * patch_cols * frames
    return pl.pallas_call(
        embed_kernel,
        out_shape=jax.ShapeDtypeStruct((frames, patch_rows * patch_cols, width), BF16),
        in_specs=[vmem()] * 4 + [pl.BlockSpec(memory_space=pl.ANY)],
        out_specs=vmem(),
        scratch_shapes=[
            pltpu.VMEM((PATCH, patch_cols, patch_rows, frames, feats), BF16),
            pltpu.VMEM(patch_w.shape, BF16),
            pltpu.VMEM((count, width), F32),
            pltpu.SemaphoreType.DMA,
        ],
        compiler_params=pltpu.CompilerParams(vmem_limit_bytes=VMEM_LIMIT),
        name="embed",
    )(tall, position, band(stem_w), jnp.tile(stem_b, PATCH)[None, :], patch_w)


def regroup_kernel(n_gx, group, src_ref, out_ref, send_sem, recv_sem, own_sem):
    frames = src_ref.shape[0]
    gy, gx = lax.axis_index("gy"), lax.axis_index("gx")
    low = lax.rem(gy, group)
    me = (gy // group) * n_gx + gx

    def device(frame):
        return ((frame // n_gx) * group + low, lax.rem(frame, n_gx))

    barrier = pltpu.get_barrier_semaphore()

    def greet(k, carry):
        pl.semaphore_signal(
            barrier, inc=1, device_id=device(lax.rem(me + k, frames)), device_id_type=MESH
        )
        return carry

    lax.fori_loop(1, frames, greet, 0)
    own = pltpu.make_async_copy(src_ref.at[me], out_ref.at[me], own_sem)
    own.start()
    pl.semaphore_wait(barrier, frames - 1)

    def copy(k):
        to = lax.rem(me + k, frames)
        return pltpu.make_async_remote_copy(
            src_ref=src_ref.at[to],
            dst_ref=out_ref.at[me],
            send_sem=send_sem.at[k],
            recv_sem=recv_sem.at[k],
            device_id=device(to),
            device_id_type=MESH,
        )

    def start(k, carry):
        copy(k).start()
        return carry

    def finish(k, carry):
        fro = lax.rem(me - k + frames, frames)
        pltpu.make_async_remote_copy(
            src_ref=src_ref.at[fro],
            dst_ref=out_ref.at[fro],
            send_sem=send_sem.at[k],
            recv_sem=recv_sem.at[k],
            device_id=device(fro),
            device_id_type=MESH,
        ).wait()
        return carry

    lax.fori_loop(1, frames, start, 0)
    lax.fori_loop(1, frames, finish, 0)
    own.wait()


def regroup(embedded, n_gx, group):
    frames = embedded.shape[0]
    return pl.pallas_call(
        functools.partial(regroup_kernel, n_gx, group),
        out_shape=jax.ShapeDtypeStruct(embedded.shape, BF16),
        in_specs=[vmem()],
        out_specs=vmem(),
        scratch_shapes=[
            pltpu.SemaphoreType.DMA((frames,)),
            pltpu.SemaphoreType.DMA((frames,)),
            pltpu.SemaphoreType.DMA,
        ],
        compiler_params=pltpu.CompilerParams(collective_id=0, has_side_effects=True),
        name="regroup",
    )(embedded)


def head_scale(tile, gain):
    left = lax.broadcasted_iota(jnp.int32, tile.shape, 1) < HEAD_DIM
    square = tile * tile
    one = jnp.sum(jnp.where(left, square, 0.0), -1, keepdims=True)
    two = jnp.sum(jnp.where(left, 0.0, square), -1, keepdims=True)
    scale = lax.rsqrt(jnp.where(left, one, two) * (1.0 / HEAD_DIM) + eps)
    return tile * scale * gain


def project_kernel(seq_ref, norm_ref, w_ref, qg_ref, kg_ref, q_ref, kv_ref):
    width = seq_ref.shape[1]
    normed = layer_norm(seq_ref[...].astype(F32), norm_ref[...]).astype(BF16)
    pair = 2 * HEAD_DIM
    for at in range(0, 3 * width, 2 * pair):
        both = jnp.dot(normed, w_ref[:, at : at + 2 * pair], preferred_element_type=F32)
        for half in range(2):
            tile = both[:, half * pair : (half + 1) * pair]
            here = at % width + half * pair
            lanes = slice(here, here + pair)
            if at < width:
                made = head_scale(tile, qg_ref[:, lanes]) * HEAD_DIM ** (-0.5)
                q_ref[:, lanes] = made.astype(BF16)
            elif at < 2 * width:
                kv_ref[0, :, lanes] = head_scale(tile, kg_ref[:, lanes]).astype(BF16)
            else:
                kv_ref[1, :, lanes] = tile.astype(BF16)


def project(seq, norm_one, qkv_w, q_gain, k_gain):
    count, width = seq.shape
    return pl.pallas_call(
        project_kernel,
        out_shape=(
            jax.ShapeDtypeStruct((count, width), BF16),
            jax.ShapeDtypeStruct((2, count, width), BF16),
        ),
        in_specs=[vmem()] * 5,
        out_specs=(vmem(), vmem()),
        compiler_params=pltpu.CompilerParams(vmem_limit_bytes=VMEM_LIMIT),
        name="project",
    )(seq, norm_one[None, :], qkv_w, q_gain[None, :], k_gain[None, :])


def share_kernel(group, src_ref, out_ref, send_sem, recv_sem, own_sem):
    gy, gx = lax.axis_index("gy"), lax.axis_index("gx")
    low = lax.rem(gy, group)
    base = gy - low

    def device(other):
        return (base + other, gx)

    barrier = pltpu.get_barrier_semaphore()

    def greet(k, carry):
        pl.semaphore_signal(
            barrier, inc=1, device_id=device(lax.rem(low + k, group)), device_id_type=MESH
        )
        return carry

    lax.fori_loop(1, group, greet, 0)
    own = pltpu.make_async_copy(src_ref, out_ref.at[low], own_sem)
    own.start()
    pl.semaphore_wait(barrier, group - 1)

    def copy(k, slot):
        return pltpu.make_async_remote_copy(
            src_ref=src_ref,
            dst_ref=out_ref.at[slot],
            send_sem=send_sem.at[k],
            recv_sem=recv_sem.at[k],
            device_id=device(lax.rem(low + k, group)),
            device_id_type=MESH,
        )

    def start(k, carry):
        copy(k, low).start()
        return carry

    def finish(k, carry):
        copy(k, lax.rem(low - k + group, group)).wait()
        return carry

    lax.fori_loop(1, group, start, 0)
    lax.fori_loop(1, group, finish, 0)
    own.wait()


def share(kv, group):
    if group == 1:
        return kv[None]
    return pl.pallas_call(
        functools.partial(share_kernel, group),
        out_shape=jax.ShapeDtypeStruct((group,) + kv.shape, BF16),
        in_specs=[vmem()],
        out_specs=vmem(),
        scratch_shapes=[
            pltpu.SemaphoreType.DMA((group,)),
            pltpu.SemaphoreType.DMA((group,)),
            pltpu.SemaphoreType.DMA,
        ],
        compiler_params=pltpu.CompilerParams(
            collective_id=1, has_side_effects=True, vmem_limit_bytes=VMEM_LIMIT
        ),
        name="share",
    )(kv)


def layer_kernel(
    seq_ref, q_ref, kv_ref, ow_ref, norm2_ref, wi_hbm, wo_hbm, last_ref, out_ref,
    attended, wi, wo, sems,
):
    count, width = seq_ref.shape
    group = kv_ref.shape[0]
    hidden = wi.shape[1]
    loads = [
        pltpu.make_async_copy(wi_hbm, wi, sems.at[0]),
        pltpu.make_async_copy(wo_hbm, wo, sems.at[1]),
    ]
    for load in loads:
        load.start()
    pair = 2 * HEAD_DIM
    block = 256

    def attend(lanes, rows):
        q = q_ref[rows, lanes]
        left = lax.broadcasted_iota(jnp.int32, q.shape, 1) < HEAD_DIM
        halves = []
        for side in range(2):
            mine = jnp.where(left if side == 0 else jnp.logical_not(left), q, jnp.zeros_like(q))
            scores = [
                lax.dot_general(
                    mine, kv_ref[g, 0, :, lanes], (((1,), (1,)), ((), ())),
                    preferred_element_type=F32,
                )
                for g in range(group)
            ]
            top = functools.reduce(
                jnp.maximum, [jnp.max(part, -1, keepdims=True) for part in scores]
            )
            totals, made = 0.0, 0.0
            for g in range(group):
                expd = jnp.exp(scores[g] - top)
                totals = totals + jnp.sum(expd, -1, keepdims=True)
                made = made + jnp.dot(
                    expd.astype(BF16), kv_ref[g, 1, :, lanes], preferred_element_type=F32
                )
            halves.append(made / totals)
        attended[rows, lanes] = jnp.where(left, halves[0], halves[1]).astype(BF16)

    depth = max(32, 2 * block // group)

    def each(step, carry):
        at = pl.multiple_of((step // (count // depth)) * pair, pair)
        low = pl.multiple_of(lax.rem(step, count // depth) * depth, depth)
        attend(pl.ds(at, pair), pl.ds(low, depth))
        return carry

    lax.fori_loop(0, (width // pair) * (count // depth), each, 0)

    for load in loads:
        load.wait()
    total = jnp.zeros((1, width), F32)
    for low in range(0, count, block):
        rows = slice(low, low + block)
        stream = seq_ref[rows, :].astype(F32) + jnp.dot(
            attended[rows, :], ow_ref[...], preferred_element_type=F32
        )
        normed = layer_norm(stream, norm2_ref[...]).astype(BF16)
        final = stream
        for at in range(0, hidden, width):
            inner = gelu(
                jnp.dot(normed, wi[:, at : at + width], preferred_element_type=F32)
            ).astype(BF16)
            final = final + jnp.dot(inner, wo[at : at + width, :], preferred_element_type=F32)
        total = total + jnp.sum(layer_norm(final, last_ref[...]), 0, keepdims=True)
    out_ref[...] = total


def layer(seq, q, kv, out_w, norm_two, mlp_in, mlp_out, norm_last):
    count, width = seq.shape
    anywhere = pl.BlockSpec(memory_space=pl.ANY)
    return pl.pallas_call(
        layer_kernel,
        out_shape=jax.ShapeDtypeStruct((1, width), F32),
        in_specs=[vmem()] * 5 + [anywhere, anywhere, vmem()],
        out_specs=vmem(),
        scratch_shapes=[
            pltpu.VMEM((count, width), BF16),
            pltpu.VMEM(mlp_in.shape, BF16),
            pltpu.VMEM(mlp_out.shape, BF16),
            pltpu.SemaphoreType.DMA((2,)),
        ],
        compiler_params=pltpu.CompilerParams(vmem_limit_bytes=VMEM_LIMIT),
        name="layer",
    )(seq, q, kv, out_w, norm_two[None, :], mlp_in, mlp_out, norm_last[None, :])


def collect_kernel(n_gx, count, src_ref, out_ref, send_sem, recv_sem, own_sem):
    gy, gx = lax.axis_index("gy"), lax.axis_index("gx")
    me = gy * n_gx + gx

    def device(other):
        return (other // n_gx, lax.rem(other, n_gx))

    barrier = pltpu.get_barrier_semaphore()

    def greet(k, carry):
        pl.semaphore_signal(
            barrier, inc=1, device_id=device(lax.rem(me + k, count)), device_id_type=MESH
        )
        return carry

    lax.fori_loop(1, count, greet, 0)
    own = pltpu.make_async_copy(src_ref, out_ref.at[me], own_sem)
    own.start()
    pl.semaphore_wait(barrier, count - 1)

    def copy(k, slot):
        return pltpu.make_async_remote_copy(
            src_ref=src_ref,
            dst_ref=out_ref.at[slot],
            send_sem=send_sem.at[k],
            recv_sem=recv_sem.at[k],
            device_id=device(lax.rem(me + k, count)),
            device_id_type=MESH,
        )

    def start(k, carry):
        copy(k, me).start()
        return carry

    def finish(k, carry):
        copy(k, lax.rem(me - k + count, count)).wait()
        return carry

    lax.fori_loop(1, count, start, 0)
    lax.fori_loop(1, count, finish, 0)
    own.wait()


def collect(partial, n_gx, count):
    return pl.pallas_call(
        functools.partial(collect_kernel, n_gx, count),
        out_shape=jax.ShapeDtypeStruct((count,) + partial.shape, F32),
        in_specs=[vmem()],
        out_specs=vmem(),
        scratch_shapes=[
            pltpu.SemaphoreType.DMA((count,)),
            pltpu.SemaphoreType.DMA((count,)),
            pltpu.SemaphoreType.DMA,
        ],
        compiler_params=pltpu.CompilerParams(collective_id=2, has_side_effects=True),
        name="collect",
    )(partial)


def critic_kernel(
    sums_ref, w_ref, b_ref, act_ref, samp_ref, targ_ref, q_ref, loss_ref, mean_ref, *, n_gx, tokens
):
    count, _, width = sums_ref.shape
    frames, actions = q_ref.shape
    group = count // frames
    rows = []
    for frame in range(frames):
        high, gx = frame // n_gx, frame % n_gx
        part = 0.0
        for low in range(group):
            part = part + sums_ref[(high * group + low) * n_gx + gx]
        rows.append(part)
    pooled = jnp.concatenate(rows, axis=0) / tokens
    q = b_ref[...] + jnp.zeros((frames, actions), F32)
    rest = pooled
    made = 0.0
    for _ in range(3):
        piece = rest.astype(BF16)
        rest = rest - piece.astype(F32)
        made = made + jnp.dot(piece, w_ref[...], preferred_element_type=F32)
    q = made + b_ref[...]
    q_ref[...] = q
    columns = lax.broadcasted_iota(jnp.int32, (frames, actions), 1)

    def pick(index):
        return jnp.sum(jnp.where(index == columns, q, 0.0), -1, keepdims=True)

    chosen = pick(act_ref[...])
    picked = [pick(samp_ref[:, s : s + 1]) for s in range(samp_ref.shape[1])]
    top = functools.reduce(jnp.maximum, picked)
    total = sum(jnp.exp(one - top) for one in picked)
    spread = top + jnp.log(total)
    loss = penalty_weight * (spread - chosen) + 0.5 * (chosen - targ_ref[...]) ** 2
    loss_ref[...] = loss
    mean_ref[...] = jnp.mean(loss, 0, keepdims=True)


def critic(sums, head_w, head_b, dataset_action, sampled, targets, n_gx, tokens):
    frames = targets.shape[0]
    q, losses, mean = pl.pallas_call(
        functools.partial(critic_kernel, n_gx=n_gx, tokens=tokens),
        out_shape=(
            jax.ShapeDtypeStruct((frames, head_w.shape[1]), F32),
            jax.ShapeDtypeStruct((frames, 1), F32),
            jax.ShapeDtypeStruct((1, 1), F32),
        ),
        in_specs=[vmem()] * 6,
        out_specs=(vmem(),) * 3,
        compiler_params=pltpu.CompilerParams(vmem_limit_bytes=VMEM_LIMIT),
        name="critic",
    )(sums, head_w, head_b[None, :], dataset_action[:, None], sampled, targets[:, None])
    return q, losses.reshape(frames), mean.reshape(())


def shards(
    images, position, stem_w, stem_b, patch_w, norm_one, qkv_w, q_gain, k_gain, out_w, norm_two,
    mlp_in, mlp_out, norm_last, head_w, head_b, dataset_action, sampled, targets,
):
    n_gy, n_gx = lax.axis_size("gy"), lax.axis_size("gx")
    frames = images.shape[0]
    group = n_gy * n_gx // frames
    assert group * frames == n_gy * n_gx and n_gy % group == 0
    embedded = embed(borders(images), position, stem_w, stem_b, patch_w)
    seq = regroup(embedded, n_gx, group).reshape(-1, embedded.shape[-1])
    q, kv = project(seq, norm_one, qkv_w, q_gain, k_gain)
    partial = layer(seq, q, share(kv, group), out_w, norm_two, mlp_in, mlp_out, norm_last)
    sums = collect(partial, n_gx, n_gy * n_gx)
    return critic(
        sums, head_w, head_b, dataset_action, sampled, targets, n_gx, seq.shape[0] * group
    )


def solution(mesh):
    in_specs = (P(None, "gy", "gx"), P("gy", "gx", None)) + (P(),) * 17
    return jax.shard_map(
        shards, mesh=mesh, in_specs=in_specs, out_specs=(P(), P(), P()), check_vma=False
    )
```

profile of v0, /device:TPU:0, one launch (start us, length us, event | category | flops | bytes accessed | tf_op | source)
XLA Modules:
  0.0 115.8 jit_solution(10864290307853677136)
XLA Ops:
  0.6 0.0 copy-start
  0.7 1.2 %copy.33 = bf16[16,56,336]{2,0,1:T(8,128)(2,1)S(1)} copy(bf16[16,56,336]{2,1,0:T(8,128)(2,1)} %param.23) | data formatting | bytes 1204224 | tf_op args[0]
  1.9 0.0 copy-start.1
  1.9 0.0 copy-start.2
  1.9 0.0 copy-start.3
  1.9 1.4 %collective-permute-start.1 = (bf16[1,16,336]{2,1,0:T(8,128)(2,1)S(1)}, bf16[1,16,336]{2,1,0:T(8,128)(2,1)S(1)}, u32[]{:S(2)}, u32[]{:S(2)}) collective-permute-start(bf16[1,16,336]{2,1,0:T(8,128)(2,1)S(1)} %get-tuple-element.16), channel_id=1, source_target_pairs={{4,0},{8,4},{12,8},{16,12},{20,16},{24,20},{28,24},{5,1},{9,5},{13... | collective-permute-start | bytes 32264 | tf_op jit(solution)/shard_map/ppermute | solution.py:44
  3.4 3.0 %collective-permute-start = (bf16[1,16,336]{2,1,0:T(8,128)(2,1)S(1)}, bf16[1,16,336]{2,1,0:T(8,128)(2,1)S(1)}, u32[]{:S(2)}, u32[]{:S(2)}) collective-permute-start(bf16[1,16,336]{2,1,0:T(8,128)(2,1)S(1)} %get-tuple-element.15), channel_id=1, source_target_pairs={{0,4},{4,8},{8,12},{12,16},{16,20},{20,24},{24,28},{1,5},{5,9},{9,... | collective-permute-start | bytes 32264 | tf_op jit(solution)/shard_map/ppermute | solution.py:43
  6.4 0.1 tile.7
  6.6 0.2 fusion.4
  6.8 0.0 copy-start.10
  6.9 0.3 collective-permute-done
  7.2 0.1 pad_maximum_fusion.3
  7.4 1.3 %collective-permute-start.3 = (bf16[58,16,3]{2,1,0:T(8,128)(2,1)S(1)}, bf16[58,16,3]{2,1,0:T(8,128)(2,1)S(1)}, u32[]{:S(2)}, u32[]{:S(2)}) collective-permute-start(bf16[58,16,3]{2,1,0:T(8,128)(2,1)S(1)} %get-tuple-element.14), channel_id=1, source_target_pairs={{1,0},{2,1},{3,2},{5,4},{6,5},{7,6},{9,8},{10,9},{11,10},{13,12},{... | collective-permute-start | bytes 16712 | tf_op jit(solution)/shard_map/ppermute | solution.py:44
  8.7 5.5 %collective-permute-start.2 = (bf16[58,16,3]{2,1,0:T(8,128)(2,1)S(1)}, bf16[58,16,3]{2,1,0:T(8,128)(2,1)S(1)}, u32[]{:S(2)}, u32[]{:S(2)}) collective-permute-start(bf16[58,16,3]{2,1,0:T(8,128)(2,1)S(1)} %get-tuple-element.13), channel_id=1, source_target_pairs={{0,1},{1,2},{2,3},{4,5},{5,6},{6,7},{8,9},{9,10},{10,11},{12,13},{... | collective-permute-start | bytes 16712 | tf_op jit(solution)/shard_map/ppermute | solution.py:43
  14.2 0.8 fusion.1.band_ref
  15.0 0.7 broadcast_in_dim_tile.3.bias_ref
  15.6 0.6 broadcast_in_dim.31.norm_ref
  16.2 0.6 broadcast_in_dim.32.qg_ref
  16.8 0.6 broadcast_in_dim.33.kg_ref
  17.4 0.6 broadcast_in_dim.34.norm2_ref
  18.0 0.6 broadcast_in_dim.35.last_ref
  18.6 0.7 copy.30.act_ref
  19.3 0.7 copy.31.targ_ref
  19.9 1.4 %pad_maximum_fusion.tall_ref = bf16[58,16,342]{2,1,0:T(8,128)(2,1)} fusion(bf16[58,16,3]{2,1,0:T(8,128)(2,1)S(1)} %collective-permute-done.3, bf16[1,16,336]{2,1,0:T(8,128)(2,1)S(1)} %collective-permute-done.1, bf16[56,16,336]{2,1,0:T(8,128)(2,1)S(1)} %bitcast.14, bf16[1,16,336]{2,1,0:T(8,128)(2,1)S(1)} %collective-permute-done, ...), kind=kLoop, calls=%fused_computation | loop fusion | flops 3173760 | bytes 1269504 | tf_op jit(solution)/shard_map/concatenate | solution.py:45
  21.3 16.6 %embed.1.src_ref = bf16[16,32,768]{2,1,0:T(8,128)(2,1)} custom-call(bf16[58,16,342]{2,1,0:T(8,128)(2,1)} %pad_maximum_fusion.tall_ref, bf16[4,8,768]{2,1,0:T(8,128)(2,1)} %pos_ref.1, bf16[144,448]{1,0:T(8,128)(2,1)} %fusion.1.band_ref, f32[1,448]{1,0:T(1,128)} %broadcast_in_dim_tile.3.bias_ref, bf16[6272,768]{1,0:T(8,128)(2,1)} %pw_hbm.1), custom_call_target="tpu_custom_call" | custom-call | tf_op jit(solution)/shard_map/embed/pallas_call | solution.py:118
  37.9 22.8 %regroup.1 = bf16[16,32,768]{2,1,0:T(8,128)(2,1)} custom-call(bf16[16,32,768]{2,1,0:T(8,128)(2,1)} %embed.1.src_ref), custom_call_target="tpu_custom_call" | custom-call | tf_op jit(solution)/shard_map/regroup/pallas_call | solution.py:190
  60.7 5.9 %project.1 = (bf16[512,768]{1,0:T(8,128)(2,1)}, bf16[2,512,768]{2,1,0:T(8,128)(2,1)}) custom-call(bf16[512,768]{1,0:T(8,128)(2,1)} %bitcast.10, f32[1,768]{1,0:T(1,128)} %broadcast_in_dim.31.norm_ref, bf16[768,2304]{1,0:T(8,128)(2,1)} %w_ref.2, f32[1,768]{1,0:T(1,128)} %broadcast_in_dim.32.qg_ref, f32[1,768]{1,0:T(1,128)} %broadcast_in_dim.33.kg_ref), custom_call_target="tpu_custom_call" | custom-call | tf_op jit(solution)/shard_map/project/pallas_call | solution.py:235
  66.6 6.5 %share.1.kv_ref = bf16[2,2,512,768]{3,2,1,0:T(8,128)(2,1)} custom-call(bf16[2,512,768]{2,1,0:T(8,128)(2,1)} %get-tuple-element.9.src_ref), custom_call_target="tpu_custom_call" | custom-call | tf_op jit(solution)/shard_map/share/pallas_call | solution.py:295
  73.1 23.7 %layer.1.src_ref = f32[1,768]{1,0:T(1,128)} custom-call(bf16[512,768]{1,0:T(8,128)(2,1)} %bitcast.11, bf16[512,768]{1,0:T(8,128)(2,1)} %get-tuple-element.8.q_ref, bf16[2,2,512,768]{3,2,1,0:T(8,128)(2,1)} %share.1.kv_ref, bf16[768,768]{1,0:T(8,128)(2,1)} %ow_ref.1, f32[1,768]{1,0:T(1,128)} %broadcast_in_dim.34.norm2_ref, bf16[768,3072]{1,0:T(8,128)(2,1)} %wi_hbm.1, ...), custom_call_target="tpu_custom_call" | custom-call | tf_op jit(solution)/shard_map/layer/pallas_call | solution.py:386
  96.8 14.8 %collect.1.sums_ref = f32[32,1,768]{2,1,0:T(1,128)} custom-call(f32[1,768]{1,0:T(1,128)} %layer.1.src_ref), custom_call_target="tpu_custom_call" | custom-call | tf_op jit(solution)/shard_map/collect/pallas_call | solution.py:446
  111.5 2.9 %critic.1 = (f32[16,1024]{1,0:T(8,128)}, f32[16,1]{1,0:T(8,128)}, f32[1,1]{1,0:T(1,128)}) custom-call(f32[32,1,768]{2,1,0:T(1,128)} %collect.1.sums_ref, bf16[768,1024]{1,0:T(8,128)(2,1)} %w_ref.3, f32[1,1024]{1,0:T(1,128)} %bitcast.15, s32[16,1]{1,0:T(8,128)} %copy.30.act_ref, s32[16,10]{1,0:T(8,128)} %samp_ref.1, f32[16,1]{1,0:T(8,128)} %copy.31.targ_ref), custom_call_target="tpu_custom_call" | custom-call | tf_op jit(solution)/shard_map/critic/pallas_call | solution.py:501
  114.4 1.3 %reduce = f32[16]{0:T(128)} reduce(f32[16,1]{1,0:T(8,128)} %get-tuple-element.11, f32[]{:T(128)} %constant.15), dimensions={1}, to_apply=%get-tuple-element.11.reduce_sub_computation | reduce | bytes 132 | tf_op jit(solution)/shard_map/critic/pallas_call | solution.py:501
  (27 shorter events, 0.1 us)
Async XLA Ops:
  0.6 5.9 %copy-start = (bf16[432,27]{1,0:T(8,128)(2,1)S(1)}, bf16[432,27]{1,0:T(8,128)(2,1)}, u32[]{:S(2)}) copy-start(bf16[432,27]{1,0:T(8,128)(2,1)} %constant.10.clone) | copy-start | bytes 69988
  0.6 5.8 %copy-start.4 = (bf16[27,32]{1,0:T(8,128)(2,1)S(1)}, bf16[27,32]{1,0:T(8,128)(2,1)}, u32[]{:S(2)}) copy-start(bf16[27,32]{1,0:T(8,128)(2,1)} %param.25) | copy-start | bytes 5188
  1.9 12.3 %copy-start.1 = (pred[144,448]{1,0:T(8,128)(4,1)S(1)}, pred[144,448]{1,0:T(8,128)(4,1)}, u32[]{:S(2)}) copy-start(pred[144,448]{1,0:T(8,128)(4,1)} %constant.13.clone) | copy-start | bytes 193540
  1.9 12.3 %copy-start.2 = (pred[144,448]{1,0:T(8,128)(4,1)S(1)}, pred[144,448]{1,0:T(8,128)(4,1)}, u32[]{:S(2)}) copy-start(pred[144,448]{1,0:T(8,128)(4,1)} %constant.12.clone) | copy-start | bytes 193540
  1.9 12.3 %copy-start.3 = (pred[144,448]{1,0:T(8,128)(4,1)S(1)}, pred[144,448]{1,0:T(8,128)(4,1)}, u32[]{:S(2)}) copy-start(pred[144,448]{1,0:T(8,128)(4,1)} %constant.11.clone) | copy-start | bytes 193540
  1.9 5.0 %collective-permute-start.1 = (bf16[1,16,336]{2,1,0:T(8,128)(2,1)S(1)}, bf16[1,16,336]{2,1,0:T(8,128)(2,1)S(1)}, u32[]{:S(2)}, u32[]{:S(2)}) collective-permute-start(bf16[1,16,336]{2,1,0:T(8,128)(2,1)S(1)} %get-tuple-element.16), channel_id=1, source_target_pairs={{4,0},{8,4},{12,8},{16,12},{20,16},{24,20},{28,24},{5,1},{9,5},{13... | collective-permute-start | bytes 32264 | tf_op jit(solution)/shard_map/ppermute | solution.py:44
  3.4 3.9 %collective-permute-start = (bf16[1,16,336]{2,1,0:T(8,128)(2,1)S(1)}, bf16[1,16,336]{2,1,0:T(8,128)(2,1)S(1)}, u32[]{:S(2)}, u32[]{:S(2)}) collective-permute-start(bf16[1,16,336]{2,1,0:T(8,128)(2,1)S(1)} %get-tuple-element.15), channel_id=1, source_target_pairs={{0,4},{4,8},{8,12},{12,16},{16,20},{20,24},{24,28},{1,5},{5,9},{9,... | collective-permute-start | bytes 32264 | tf_op jit(solution)/shard_map/ppermute | solution.py:43
  6.8 8.1 %copy-start.10 = (f32[32]{0:T(128)S(1)}, f32[32]{0:T(128)}, u32[]{:S(2)}) copy-start(f32[32]{0:T(128)} %param.26) | copy-start | bytes 388
  6.8 8.8 %copy-start.5 = (f32[768]{0:T(1024)S(1)}, f32[768]{0:T(1024)}, u32[]{:S(2)}) copy-start(f32[768]{0:T(1024)} %param.28) | copy-start | bytes 9220
  6.8 9.4 %copy-start.6 = (f32[768]{0:T(1024)S(1)}, f32[768]{0:T(1024)}, u32[]{:S(2)}) copy-start(f32[768]{0:T(1024)} %param.30) | copy-start | bytes 9220
  6.9 10.0 %copy-start.7 = (f32[768]{0:T(1024)S(1)}, f32[768]{0:T(1024)}, u32[]{:S(2)}) copy-start(f32[768]{0:T(1024)} %param.31) | copy-start | bytes 9220
  6.9 10.5 %copy-start.8 = (f32[768]{0:T(1024)S(1)}, f32[768]{0:T(1024)}, u32[]{:S(2)}) copy-start(f32[768]{0:T(1024)} %param.33) | copy-start | bytes 9220
  6.9 11.1 %copy-start.9 = (f32[768]{0:T(1024)S(1)}, f32[768]{0:T(1024)}, u32[]{:S(2)}) copy-start(f32[768]{0:T(1024)} %param.36) | copy-start | bytes 9220
  6.9 11.7 %copy-start.11 = (s32[16]{0:T(128)S(1)}, s32[16]{0:T(128)}, u32[]{:S(2)}) copy-start(s32[16]{0:T(128)} %param.39) | copy-start | bytes 196
  6.9 12.3 %copy-start.12 = (f32[16]{0:T(128)S(1)}, f32[16]{0:T(128)}, u32[]{:S(2)}) copy-start(f32[16]{0:T(128)} %param.41) | copy-start | bytes 196
  7.4 12.6 %collective-permute-start.3 = (bf16[58,16,3]{2,1,0:T(8,128)(2,1)S(1)}, bf16[58,16,3]{2,1,0:T(8,128)(2,1)S(1)}, u32[]{:S(2)}, u32[]{:S(2)}) collective-permute-start(bf16[58,16,3]{2,1,0:T(8,128)(2,1)S(1)} %get-tuple-element.14), channel_id=1, source_target_pairs={{1,0},{2,1},{3,2},{5,4},{6,5},{7,6},{9,8},{10,9},{11,10},{13,12},{... | collective-permute-start | bytes 16712 | tf_op jit(solution)/shard_map/ppermute | solution.py:44
  8.7 11.3 %collective-permute-start.2 = (bf16[58,16,3]{2,1,0:T(8,128)(2,1)S(1)}, bf16[58,16,3]{2,1,0:T(8,128)(2,1)S(1)}, u32[]{:S(2)}, u32[]{:S(2)}) collective-permute-start(bf16[58,16,3]{2,1,0:T(8,128)(2,1)S(1)} %get-tuple-element.13), channel_id=1, source_target_pairs={{0,1},{1,2},{2,3},{4,5},{5,6},{6,7},{8,9},{9,10},{10,11},{12,13},{... | collective-permute-start | bytes 16712 | tf_op jit(solution)/shard_map/ppermute | solution.py:43
where the time goes:
time: 116 us
  Pallas kernels  93.1 us (80%)
  starting transfers between devices  11.2 us (10%)
  local copies, waits for them, and re-layouts  6.4 us (6%)
  other arithmetic  3.62 us (3%)
    pallas_call x1, Pallas kernels, layer(): pl.pallas_call(layer_kernel, out_shape=jax.ShapeDtypeStruct((1, width), F...  23.7 us
    pallas_call x1, Pallas kernels, regroup(): pl.pallas_call(functools.partial(regroup_kernel, n_gx, group), out_shape=...  22.8 us
    pallas_call x1, Pallas kernels, embed(): pl.pallas_call(embed_kernel, out_shape=jax.ShapeDtypeStruct((frames, patc...  16.6 us
    pallas_call x1, Pallas kernels, collect(): pl.pallas_call(functools.partial(collect_kernel, n_gx, count), out_shape=...  14.8 us
    ppermute x2, starting transfers between devices, borders(): before = lax.ppermute(tail, axis, [(i, i + 1) for i in range(ends)])  8.52 us
    pallas_call x1, Pallas kernels, share(): pl.pallas_call(functools.partial(share_kernel, group), out_shape=jax.Shap...  6.51 us
    pallas_call x1, Pallas kernels, project(): pl.pallas_call(project_kernel, out_shape=(jax.ShapeDtypeStruct((count, wi...  5.87 us
    pallas_call x1, Pallas kernels, critic(): pl.pallas_call(functools.partial(critic_kernel, n_gx=n_gx, tokens=tokens)...  2.9 us
  transfers between devices with their start and end apart: 4, of which 1 were waited for; matrix products, arithmetic and copies ran while one was open for 5% of the time, Pallas kernels for 0%

commit v1 on v0

v1 whole, which is shorter than its diff:
```python
import functools

import jax
import jax.numpy as jnp
import numpy as np
from jax import lax
from jax.experimental import pallas as pl
from jax.experimental.pallas import tpu as pltpu
from jax.sharding import PartitionSpec as P

HEAD_DIM = 64
PATCH = 14
eps = 1e-06
penalty_weight = 1.0
F32 = jnp.float32
BF16 = jnp.bfloat16
MESH = pl.DeviceIdType.MESH
VMEM_LIMIT = 56 * 1024 * 1024


def vmem():
    return pl.BlockSpec(memory_space=pltpu.VMEM)


def gelu(x):
    u = x * (0.7978845608028654 + (0.7978845608028654 * 0.044715) * (x * x))
    half = 0.5 * x
    return half + half * jnp.tanh(u)


def layer_norm(values, gain):
    centre = values - jnp.mean(values, -1, keepdims=True)
    spread = jnp.mean(centre * centre, -1, keepdims=True)
    return centre * lax.rsqrt(spread + eps) * gain


def band(stem_w):
    channels = stem_w.shape[1]
    rows = np.arange(9 * (PATCH + 2))
    row_off, rest = rows // (3 * (PATCH + 2)), rows % (3 * (PATCH + 2))
    col_in, colour = rest // 3, rest % 3
    col_out = np.arange(PATCH * channels) // channels
    wide = jnp.tile(stem_w, (1, PATCH))
    picks = np.zeros((3, rows.size, 27), np.float32)
    for col_off in range(3):
        picks[col_off, rows, row_off * 9 + col_off * 3 + colour] = 1
    spread = jnp.dot(jnp.asarray(picks.reshape(-1, 27), BF16), wide, preferred_element_type=F32)
    spread = spread.reshape(3, rows.size, -1)
    total = 0.0
    for col_off in range(3):
        keep = col_in[:, None] == col_out[None, :] + col_off
        total = total + jnp.where(keep, spread[col_off], 0.0)
    return total.astype(BF16)


def frames_kernel(
    n_gy, n_gx, group, tall_ref, pos_ref, band_ref, bias_ref, pw_hbm, out_ref,
    ext, row_in, edge_out, edge_in, stem, pw, acc, made, load_sem, side_send, side_recv, send_sem,
    recv_sem,
):
    rows, frames, lanes = tall_ref.shape
    patch_rows, patch_cols, width = pos_ref.shape
    feats = band_ref.shape[1]
    reach = 3 * (PATCH + 2)
    parts = made.shape[0]
    part_cols = patch_cols // parts
    tiles = part_cols * patch_rows
    count = tiles * frames
    gy, gx = lax.axis_index("gy"), lax.axis_index("gx")
    low = lax.rem(gy, group)
    me = (gy // group) * n_gx + gx
    load = pltpu.make_async_copy(pw_hbm, pw, load_sem)
    load.start()

    def device(frame):
        return ((frame // n_gx) * group + low, lax.rem(frame, n_gx))

    above = (lax.rem(gy + n_gy - 1, n_gy), gx)
    below = (lax.rem(gy + 1, n_gy), gx)
    before = (gy, lax.rem(gx + n_gx - 1, n_gx))
    after = (gy, lax.rem(gx + 1, n_gx))
    barrier = pltpu.get_barrier_semaphore()
    for side in (above, below, before, after):
        pl.semaphore_signal(barrier, inc=1, device_id=side, device_id_type=MESH)

    def greet(k, carry):
        pl.semaphore_signal(
            barrier, inc=1, device_id=device(lax.rem(me + k, frames)), device_id_type=MESH
        )
        return carry

    lax.fori_loop(1, frames, greet, 0)
    pl.semaphore_wait(barrier, frames + 3)

    def side_copy(k, src, dst, side):
        return pltpu.make_async_remote_copy(
            src_ref=src, dst_ref=dst, send_sem=side_send.at[k], recv_sem=side_recv.at[k],
            device_id=side, device_id_type=MESH,
        )

    vertical = [
        side_copy(0, tall_ref.at[rows - 1], row_in.at[0], below),
        side_copy(1, tall_ref.at[0], row_in.at[1], above),
    ]
    for one in vertical:
        one.start()
    ext[1 : rows + 1] = tall_ref[...]
    for one in vertical:
        one.wait()
    ext[0] = jnp.where(gy > 0, row_in[0], jnp.zeros_like(row_in[0]))
    ext[rows + 1] = jnp.where(gy < n_gy - 1, row_in[1], jnp.zeros_like(row_in[1]))
    edge_out[0] = jnp.concatenate([ext[r, :, lanes - 3 :] for r in range(rows + 2)], axis=-1)
    edge_out[1] = jnp.concatenate([ext[r, :, :3] for r in range(rows + 2)], axis=-1)
    level = [
        side_copy(2, edge_out.at[0], edge_in.at[0], after),
        side_copy(3, edge_out.at[1], edge_in.at[1], before),
    ]
    for one in level:
        one.start()

    def edge(k, inside):
        got = edge_in[k]
        got = jnp.where(inside, got, jnp.zeros_like(got))
        return jnp.stack([got[:, 3 * r : 3 * r + 3] for r in range(rows + 2)], axis=0)

    order = list(range(1, patch_cols - 1)) + [0, patch_cols - 1]
    for part in range(parts):
        for spot in range(part_cols):
            col = order[part * part_cols + spot]
            if col == 0:
                for one in level:
                    one.wait()
                cut = jnp.concatenate([edge(0, gx > 0), ext[:, :, : reach - 3]], axis=-1)
            elif col == patch_cols - 1:
                cut = jnp.concatenate(
                    [ext[:, :, lanes - reach + 3 :], edge(1, gx < n_gx - 1)], axis=-1
                )
            else:
                at = 3 * PATCH * col - 3
                cut = ext[:, :, at : at + reach]
            taps = jnp.concatenate([cut[off : off + rows] for off in range(3)], axis=-1)
            for i in range(patch_rows):
                piece = taps[i * PATCH : (i + 1) * PATCH].reshape(PATCH * frames, 3 * reach)
                conv = jnp.dot(piece, band_ref[...], preferred_element_type=F32)
                stem[:, spot, i] = (
                    gelu(conv + bias_ref[...]).astype(BF16).reshape(PATCH, frames, feats)
                )
        if part == 0:
            load.wait()
        acc[...] = jnp.zeros_like(acc)

        def step(p, carry):
            acc[...] += jnp.dot(
                stem[p].reshape(count, feats),
                pw[pl.ds(pl.multiple_of(p * feats, 64), feats), :],
                preferred_element_type=F32,
            )
            return carry

        lax.fori_loop(0, PATCH, step, 0)
        pieces = []
        for spot in range(part_cols):
            col = order[part * part_cols + spot]
            for i in range(patch_rows):
                at = (spot * patch_rows + i) * frames
                place = pos_ref[i, col : col + 1, :].astype(F32)
                pieces.append((acc[at : at + frames, :] + place).astype(BF16))
        to = lax.broadcasted_iota(jnp.int32, (count, count), 0)
        fro = lax.broadcasted_iota(jnp.int32, (count, count), 1)
        swap = jnp.where((to % tiles) * frames + to // tiles == fro, 1.0, 0.0).astype(BF16)
        made[part] = (
            jnp.dot(swap, jnp.concatenate(pieces, axis=0), preferred_element_type=F32)
            .astype(BF16)
            .reshape(frames, tiles, width)
        )

        def start(k, carry):
            to = lax.rem(me + k, frames)
            pltpu.make_async_remote_copy(
                src_ref=made.at[part, to], dst_ref=out_ref.at[me, part],
                send_sem=send_sem.at[part, k], recv_sem=recv_sem.at[part, k],
                device_id=device(to), device_id_type=MESH,
            ).start()
            return carry

        lax.fori_loop(1, frames, start, 0)
        out_ref[me, part] = made[part, me]

    for part in range(parts):

        def finish(k, carry):
            fro = lax.rem(me - k + frames, frames)
            pltpu.make_async_remote_copy(
                src_ref=made.at[part, fro], dst_ref=out_ref.at[fro, part],
                send_sem=send_sem.at[part, k], recv_sem=recv_sem.at[part, k],
                device_id=device(fro), device_id_type=MESH,
            ).wait()
            return carry

        lax.fori_loop(1, frames, finish, 0)


def own_frames(images, position, stem_w, stem_b, patch_w, n_gy, n_gx, group):
    tall = jnp.transpose(images, (1, 0, 2))
    rows, frames, lanes = tall.shape
    patch_rows, patch_cols, width = position.shape
    feats = PATCH * stem_w.shape[1]
    parts = max(1, patch_rows * patch_cols // 16)
    tiles = patch_rows * patch_cols // parts
    edges = 3 * (rows + 2)
    return pl.pallas_call(
        functools.partial(frames_kernel, n_gy, n_gx, group),
        out_shape=jax.ShapeDtypeStruct((frames, parts, tiles, width), BF16),
        in_specs=[vmem()] * 4 + [pl.BlockSpec(memory_space=pl.ANY)],
        out_specs=vmem(),
        scratch_shapes=[
            pltpu.VMEM((rows + 2, frames, lanes), BF16),
            pltpu.VMEM((2, frames, lanes), BF16),
            pltpu.VMEM((2, frames, edges), BF16),
            pltpu.VMEM((2, frames, edges), BF16),
            pltpu.VMEM((PATCH, patch_cols // parts, patch_rows, frames, feats), BF16),
            pltpu.VMEM(patch_w.shape, BF16),
            pltpu.VMEM((tiles * frames, width), F32),
            pltpu.VMEM((parts, frames, tiles, width), BF16),
            pltpu.SemaphoreType.DMA,
            pltpu.SemaphoreType.DMA((4,)),
            pltpu.SemaphoreType.DMA((4,)),
            pltpu.SemaphoreType.DMA((parts, frames)),
            pltpu.SemaphoreType.DMA((parts, frames)),
        ],
        compiler_params=pltpu.CompilerParams(
            collective_id=0, has_side_effects=True, vmem_limit_bytes=VMEM_LIMIT
        ),
        name="own_frames",
    )(tall, position, band(stem_w), jnp.tile(stem_b, PATCH)[None, :], patch_w)


def head_scale(tile, gain):
    left = lax.broadcasted_iota(jnp.int32, tile.shape, 1) < HEAD_DIM
    square = tile * tile
    one = jnp.sum(jnp.where(left, square, 0.0), -1, keepdims=True)
    two = jnp.sum(jnp.where(left, 0.0, square), -1, keepdims=True)
    scale = lax.rsqrt(jnp.where(left, one, two) * (1.0 / HEAD_DIM) + eps)
    return tile * scale * gain


def critic_kernel(
    n_gx, group, devices, tokens, seq_ref, norm_ref, w_ref, qg_ref, kg_ref, norm2_ref, last_ref,
    b_ref, act_ref, samp_ref, targ_ref, ow_hbm, wi_hbm, wo_hbm, hw_hbm, out_ref, loss_ref, mean_ref,
    q_ref, kv_ref, attended, ow, wi, wo, hw, sums, load_sem, kv_send, kv_recv, send_sem, recv_sem,
):
    count, width = seq_ref.shape
    hidden = wi.shape[1]
    frames, actions = out_ref.shape
    pair = 2 * HEAD_DIM
    loads = [
        pltpu.make_async_copy(ow_hbm, ow, load_sem.at[0]),
        pltpu.make_async_copy(wi_hbm, wi, load_sem.at[1]),
        pltpu.make_async_copy(wo_hbm, wo, load_sem.at[2]),
        pltpu.make_async_copy(hw_hbm, hw, load_sem.at[3]),
    ]
    for load in loads:
        load.start()
    gy, gx = lax.axis_index("gy"), lax.axis_index("gx")
    low = lax.rem(gy, group)
    base = gy - low
    me = gy * n_gx + gx

    def device(other):
        return (other // n_gx, lax.rem(other, n_gx))

    barrier = pltpu.get_barrier_semaphore()

    def greet(k, carry):
        pl.semaphore_signal(
            barrier, inc=1, device_id=device(lax.rem(me + k, devices)), device_id_type=MESH
        )
        return carry

    lax.fori_loop(1, devices, greet, 0)

    def kv_copy(k, which, slot):
        return pltpu.make_async_remote_copy(
            src_ref=kv_ref.at[slot, which], dst_ref=kv_ref.at[slot, which],
            send_sem=kv_send.at[which, k], recv_sem=kv_recv.at[which, k],
            device_id=(base + lax.rem(low + k, group), gx), device_id_type=MESH,
        )

    def kv_start(which):
        def start(k, carry):
            kv_copy(k, which, low).start()
            return carry

        lax.fori_loop(1, group, start, 0)

    def kv_finish(which):
        def finish(k, carry):
            kv_copy(k, which, lax.rem(low - k + group, group)).wait()
            return carry

        lax.fori_loop(1, group, finish, 0)

    normed = layer_norm(seq_ref[...].astype(F32), norm_ref[...].reshape(1, width)).astype(BF16)
    q_gain = qg_ref[...].reshape(1, width)
    k_gain = kg_ref[...].reshape(1, width)

    def project(block):
        for at in range(0, width, 2 * pair):
            both = jnp.dot(
                normed,
                w_ref[:, block * width + at : block * width + at + 2 * pair],
                preferred_element_type=F32,
            )
            for half in range(2):
                tile = both[:, half * pair : (half + 1) * pair]
                lanes = slice(at + half * pair, at + half * pair + pair)
                if block == 0:
                    scaled = head_scale(tile, q_gain[:, lanes]) * HEAD_DIM ** (-0.5)
                    q_ref[:, lanes] = scaled.astype(BF16)
                elif block == 1:
                    kv_ref[low, 0, :, lanes] = head_scale(tile, k_gain[:, lanes]).astype(BF16)
                else:
                    kv_ref[low, 1, :, lanes] = tile.astype(BF16)

    project(2)
    pl.semaphore_wait(barrier, devices - 1)
    kv_start(1)
    project(1)
    kv_start(0)
    project(0)
    kv_finish(1)
    kv_finish(0)

    def attend(lanes, rows):
        q = q_ref[rows, lanes]
        left = lax.broadcasted_iota(jnp.int32, q.shape, 1) < HEAD_DIM
        halves = []
        for side in range(2):
            mine = jnp.where(left if side == 0 else jnp.logical_not(left), q, jnp.zeros_like(q))
            scores = [
                lax.dot_general(
                    mine, kv_ref[g, 0, :, lanes], (((1,), (1,)), ((), ())),
                    preferred_element_type=F32,
                )
                for g in range(group)
            ]
            top = functools.reduce(
                jnp.maximum, [jnp.max(part, -1, keepdims=True) for part in scores]
            )
            totals, mixed = 0.0, 0.0
            for g in range(group):
                expd = jnp.exp(scores[g] - top)
                totals = totals + jnp.sum(expd, -1, keepdims=True)
                mixed = mixed + jnp.dot(
                    expd.astype(BF16), kv_ref[g, 1, :, lanes], preferred_element_type=F32
                )
            halves.append(mixed / totals)
        attended[rows, lanes] = jnp.where(left, halves[0], halves[1]).astype(BF16)

    depth = max(32, 512 // group)

    def each(step, carry):
        at = pl.multiple_of((step // (count // depth)) * pair, pair)
        first = pl.multiple_of(lax.rem(step, count // depth) * depth, depth)
        attend(pl.ds(at, pair), pl.ds(first, depth))
        return carry

    lax.fori_loop(0, (width // pair) * (count // depth), each, 0)

    for load in loads:
        load.wait()
    block = 256
    total = jnp.zeros((1, width), F32)
    for first in range(0, count, block):
        rows = slice(first, first + block)
        stream = seq_ref[rows, :].astype(F32) + jnp.dot(
            attended[rows, :], ow[...], preferred_element_type=F32
        )
        normed2 = layer_norm(stream, norm2_ref[...].reshape(1, width)).astype(BF16)
        final = stream
        for at in range(0, hidden, width):
            inner = gelu(
                jnp.dot(normed2, wi[:, at : at + width], preferred_element_type=F32)
            ).astype(BF16)
            final = final + jnp.dot(inner, wo[at : at + width, :], preferred_element_type=F32)
        total = total + jnp.sum(
            layer_norm(final, last_ref[...].reshape(1, width)), 0, keepdims=True
        )
    sums[me] = total

    def sum_copy(k, slot):
        return pltpu.make_async_remote_copy(
            src_ref=sums.at[slot], dst_ref=sums.at[slot],
            send_sem=send_sem.at[k], recv_sem=recv_sem.at[k],
            device_id=device(lax.rem(me + k, devices)), device_id_type=MESH,
        )

    def start(k, carry):
        sum_copy(k, me).start()
        return carry

    def finish(k, carry):
        sum_copy(k, lax.rem(me - k + devices, devices)).wait()
        return carry

    lax.fori_loop(1, devices, start, 0)
    lax.fori_loop(1, devices, finish, 0)

    pieces = []
    for frame in range(frames):
        part = 0.0
        for other in range(group):
            part = part + sums[((frame // n_gx) * group + other) * n_gx + frame % n_gx]
        pieces.append(part)
    rest = jnp.concatenate(pieces, axis=0) / tokens
    q = 0.0
    for _ in range(3):
        piece = rest.astype(BF16)
        rest = rest - piece.astype(F32)
        q = q + jnp.dot(piece, hw[...], preferred_element_type=F32)
    q = q + b_ref[...].reshape(1, actions)
    out_ref[...] = q
    columns = lax.broadcasted_iota(jnp.int32, (frames, actions), 1)
    same = lax.broadcasted_iota(jnp.int32, (frames, frames), 0) == lax.broadcasted_iota(
        jnp.int32, (frames, frames), 1
    )

    def upright(row):
        return jnp.sum(jnp.where(same, row.astype(F32).reshape(1, frames), 0.0), -1, keepdims=True)

    def pick(index):
        return jnp.sum(jnp.where(index == columns, q, 0.0), -1, keepdims=True)

    chosen = pick(upright(act_ref[...]).astype(jnp.int32))
    picked = [pick(samp_ref[:, s : s + 1]) for s in range(samp_ref.shape[1])]
    top = functools.reduce(jnp.maximum, picked)
    spread = top + jnp.log(sum(jnp.exp(one - top) for one in picked))
    loss = penalty_weight * (spread - chosen) + 0.5 * (chosen - upright(targ_ref[...])) ** 2
    loss_ref[...] = jnp.sum(jnp.where(same, loss, 0.0), 0, keepdims=True)
    mean_ref[...] = jnp.mean(loss, 0, keepdims=True)


def critic(
    seq, norm_one, qkv_w, q_gain, k_gain, norm_two, norm_last, head_b, dataset_action, sampled,
    targets, out_w, mlp_in, mlp_out, head_w, n_gx, group, devices,
):
    count, width = seq.shape
    frames = targets.shape[0]
    q, losses, mean = pl.pallas_call(
        functools.partial(critic_kernel, n_gx, group, devices, count * group),
        out_shape=(
            jax.ShapeDtypeStruct((frames, head_w.shape[1]), F32),
            jax.ShapeDtypeStruct((1, frames), F32),
            jax.ShapeDtypeStruct((1, 1), F32),
        ),
        in_specs=[vmem()] * 11 + [pl.BlockSpec(memory_space=pl.ANY)] * 4,
        out_specs=(vmem(),) * 3,
        scratch_shapes=[
            pltpu.VMEM((count, width), BF16),
            pltpu.VMEM((group, 2, count, width), BF16),
            pltpu.VMEM((count, width), BF16),
            pltpu.VMEM(out_w.shape, BF16),
            pltpu.VMEM(mlp_in.shape, BF16),
            pltpu.VMEM(mlp_out.shape, BF16),
            pltpu.VMEM(head_w.shape, BF16),
            pltpu.VMEM((devices, 1, width), F32),
            pltpu.SemaphoreType.DMA((4,)),
            pltpu.SemaphoreType.DMA((2, group)),
            pltpu.SemaphoreType.DMA((2, group)),
            pltpu.SemaphoreType.DMA((devices,)),
            pltpu.SemaphoreType.DMA((devices,)),
        ],
        compiler_params=pltpu.CompilerParams(
            collective_id=1, has_side_effects=True, vmem_limit_bytes=VMEM_LIMIT
        ),
        name="critic",
    )(
        seq, norm_one, qkv_w, q_gain, k_gain, norm_two, norm_last, head_b, dataset_action, sampled,
        targets, out_w, mlp_in, mlp_out, head_w,
    )
    return q, losses.reshape(frames), mean.reshape(())


def shards(
    images, position, stem_w, stem_b, patch_w, norm_one, qkv_w, q_gain, k_gain, out_w, norm_two,
    mlp_in, mlp_out, norm_last, head_w, head_b, dataset_action, sampled, targets,
):
    n_gy, n_gx = lax.axis_size("gy"), lax.axis_size("gx")
    group = n_gy * n_gx // images.shape[0]
    assert group * images.shape[0] == n_gy * n_gx and n_gy % group == 0
    embedded = own_frames(images, position, stem_w, stem_b, patch_w, n_gy, n_gx, group)
    return critic(
        embedded.reshape(-1, embedded.shape[-1]), norm_one, qkv_w, q_gain, k_gain, norm_two,
        norm_last, head_b, dataset_action, sampled, targets, out_w, mlp_in, mlp_out, head_w,
        n_gx, group, n_gy * n_gx,
    )


def solution(mesh):
    in_specs = (P(None, "gy", "gx"), P("gy", "gx", None)) + (P(),) * 17
    return jax.shard_map(
        shards, mesh=mesh, in_specs=in_specs, out_specs=(P(), P(), P()), check_vma=False
    )
```

time: 116 us -> 87.6 us (0.76)
  Pallas kernels: 93.1 us -> 75.1 us
  starting transfers between devices: 11.2 us -> 0 us
  other arithmetic: 3.62 us -> 1.75 us
  between operations: 0.89 us -> 2.35 us
    pallas_call x7 -> x2, Pallas kernels: 93.1 us -> 75.1 us  [the longest x1 39 us: critic(): pl.pallas_call(functools.partial(critic_kernel, n_gx, group, devices, cou...]
    ppermute x4 -> x0, starting transfers between devices: 11.2 us -> none  [the longest x2 8.52 us: borders(): before = lax.ppermute(tail, axis, [(i, i + 1) for i in range(ends)])]
    broadcast_in_dim x7 -> x0, local copies, waits for them, and re-layouts: 4.28 us -> none  [the longest x1 0.67 us: critic(): targets[:, None]]
    unnamed x27 -> x3, local copies, waits for them, and re-layouts: 1.31 us -> 4.7 us
    concatenate x1 -> x0, other arithmetic: 1.38 us -> none  [borders(): tall = jnp.concatenate([before, tall, after], axis=dim)]
    pallas_call x1 -> x0, other arithmetic: 1.32 us -> none  [critic(): pl.pallas_call(functools.partial(critic_kernel, n_gx=n_gx, tokens=tokens)...]
  transfers between devices with their start and end apart: 4 -> 0, of which waited for: 1 -> 0; matrix products, arithmetic and copies ran while one was open for 5% -> 0% of each run, Pallas kernels for 0% -> 0%
where the time goes in v1:
time: 87.6 us; the launch traced here: 87.2 us
  Pallas kernels  75.1 us (86%)
  local copies, waits for them, and re-layouts  6.86 us (8%)
  between operations  2.35 us (3%)
  other arithmetic  1.75 us (2%)
  matrix products  1.13 us (1%)
    pallas_call x1, Pallas kernels, critic(): pl.pallas_call(functools.partial(critic_kernel, n_gx, group, devices, cou...  39 us
    pallas_call x1, Pallas kernels, own_frames(): pl.pallas_call(functools.partial(frames_kernel, n_gy, n_gx, group), out_s...  36.1 us
    unnamed x3, local copies, waits for them, and re-layouts  4.7 us
    convert_element_type x1, other arithmetic, band(): return total.astype(BF16)  1.75 us

profile of v1, /device:TPU:0, one launch (start us, length us, event | category | flops | bytes accessed | tf_op | source)
XLA Modules:
  0.0 87.2 jit_solution(10406992325805710127)
XLA Ops:
  0.6 0.7 tile.6
  1.3 0.1 tile.7
  1.5 1.1 %fusion.3 = f32[432,448]{1,0:T(8,128)S(1)} fusion(bf16[432,27]{1,0:T(8,128)(2,1)} %constant.10.clone, bf16[27,448]{1,0:T(8,128)(2,1)S(1)} %tile.7), kind=kOutput, calls=%fused_computation.7 | convolution fusion | flops 10450944 | bytes 821664 | tf_op jit(solution)/shard_map/dot_general | solution.py:47
  2.6 1.8 %fusion.1.band_ref = bf16[144,448]{1,0:T(8,128)(2,1)} fusion(pred[144,448]{1,0:T(8,128)(4,1)} %constant.13.clone, f32[432,448]{1,0:T(8,128)S(1)} %fusion.3, pred[144,448]{1,0:T(8,128)(4,1)} %constant.12.clone, pred[144,448]{1,0:T(8,128)(4,1)} %constant.11.clone), kind=kLoop, calls=%fused_computation.3 | loop fusion | flops 387072 | bytes 1096704 | tf_op jit(solution)/shard_map/convert_element_type | solution.py:53
  4.4 2.1 %copy.28 = bf16[16,56,336]{2,0,1:T(8,128)(2,1)} copy(bf16[16,56,336]{2,1,0:T(8,128)(2,1)} %param.23) | data formatting | bytes 1204224 | tf_op args[0]
  6.4 0.7 tile.8
  7.1 0.7 broadcast_in_dim_tile.3.bias_ref
  7.7 36.1 %own_frames.1 = bf16[16,2,16,768]{3,2,1,0:T(8,128)(2,1)} custom-call(bf16[56,16,336]{2,1,0:T(8,128)(2,1)} %bitcast.9, bf16[4,8,768]{2,1,0:T(8,128)(2,1)} %pos_ref.1, bf16[144,448]{1,0:T(8,128)(2,1)} %fusion.1.band_ref, f32[1,448]{1,0:T(1,128)} %broadcast_in_dim_tile.3.bias_ref, bf16[6272,768]{1,0:T(8,128)(2,1)} %pw_hbm.1), custom_call_target="tpu_custom_call" | custom-call | tf_op jit(solution)/shard_map/own_frames/pallas_call | solution.py:211
  43.8 39.0 %critic.1 = (f32[16,1024]{1,0:T(8,128)}, f32[1,16]{1,0:T(1,128)}, f32[1,1]{1,0:T(1,128)}) custom-call(bf16[512,768]{1,0:T(8,128)(2,1)} %bitcast.8, f32[768]{0:T(1024)} %norm_ref.1, bf16[768,2304]{1,0:T(8,128)(2,1)} %w_ref.1, f32[768]{0:T(1024)} %qg_ref.1, f32[768]{0:T(1024)} %kg_ref.1, f32[768]{0:T(1024)} %norm2_ref.1, f32[768]{0:T(1024)} %last_ref.1, ...), custom_call_target="tpu_custom_call" | custom-call | tf_op jit(solution)/shard_map/critic/pallas_call | solution.py:449
  82.9 1.5 %copy.32 = f32[16,1024]{1,0:T(8,128)} copy(f32[16,1024]{1,0:T(8,128)} %get-tuple-element.12) | data formatting | bytes 131072
  84.4 1.2 %copy.33 = f32[16]{0:T(128)} copy(f32[16]{0:T(128)} %bitcast.10) | data formatting | bytes 128

commit v2 on v1

v2 whole, which is shorter than its diff:
```python
import functools

import jax
import jax.numpy as jnp
from jax import lax
from jax.experimental import pallas as pl
from jax.experimental.pallas import tpu as pltpu
from jax.sharding import PartitionSpec as P

HEAD_DIM = 64
PATCH = 14
eps = 1e-06
penalty_weight = 1.0
F32 = jnp.float32
BF16 = jnp.bfloat16
MESH = pl.DeviceIdType.MESH
VMEM_LIMIT = 60 * 1024 * 1024


def vmem():
    return pl.BlockSpec(memory_space=pltpu.VMEM)


def gelu(x):
    u = x * (0.7978845608028654 + (0.7978845608028654 * 0.044715) * (x * x))
    half = 0.5 * x
    return half + half * jnp.tanh(u)


def layer_norm(values, gain):
    centre = values - jnp.mean(values, -1, keepdims=True)
    spread = jnp.mean(centre * centre, -1, keepdims=True)
    return centre * lax.rsqrt(spread + eps) * gain


def band(stem_w, length):
    wide = jnp.concatenate([stem_w] * length, axis=-1)
    channels = stem_w.shape[1]
    reach = 3 * (length + 2)

    def grid(shape):
        return [lax.broadcasted_iota(jnp.int32, shape, axis) for axis in range(2)]

    row, tap = grid((3 * reach, 27))
    place, lane = grid((3 * reach, length * channels))
    total = 0.0
    for off in range(3):
        picks = tap == (row // reach) * 9 + off * 3 + row % 3
        spread = jnp.dot(
            jnp.where(picks, 1.0, 0.0).astype(BF16), wide, preferred_element_type=F32
        )
        total = total + jnp.where((place % reach) // 3 == lane // channels + off, spread, 0.0)
    return total.astype(BF16)


def head_scale(tile, gain):
    left = lax.broadcasted_iota(jnp.int32, tile.shape, 1) < HEAD_DIM
    square = tile * tile
    one = jnp.sum(jnp.where(left, square, 0.0), -1, keepdims=True)
    two = jnp.sum(jnp.where(left, 0.0, square), -1, keepdims=True)
    scale = lax.rsqrt(jnp.where(left, one, two) * (1.0 / HEAD_DIM) + eps)
    return tile * scale * gain


def whole_kernel(
    n_gy, n_gx, group, tall_ref, pos_ref, sw_ref, sb_ref, norm_ref, qg_ref, kg_ref, norm2_ref,
    last_ref, b_ref, act_ref, samp_ref, targ_ref, pw_hbm, qkv_hbm, ow_hbm, wi_hbm, wo_hbm, hw_hbm,
    out_ref, loss_ref, mean_ref, ext, row_in, edge_out, edge_in, band_ref, stem, pw, acc, made, got,
    q_ref, kv_ref, attended, w_ref, ow, wi, wo, hw, sums, load_sem, side_send, side_recv, send_sem,
    recv_sem, kv_send, kv_recv, sum_send, sum_recv,
):
    rows, frames, lanes = tall_ref.shape
    patch_rows, patch_cols, width = pos_ref.shape
    feats = band_ref.shape[1]
    pair = 2 * HEAD_DIM
    hidden = wi.shape[1]
    actions = out_ref.shape[1]
    devices = n_gy * n_gx
    reach = 3 * (PATCH + 2)
    parts = made.shape[0]
    part_cols = patch_cols // parts
    tiles = part_cols * patch_rows
    part_count = tiles * frames
    gy, gx = lax.axis_index("gy"), lax.axis_index("gx")
    low = lax.rem(gy, group)
    slot = (gy // group) * n_gx + gx
    pw_load = pltpu.make_async_copy(pw_hbm, pw, load_sem.at[0])
    pw_load.start()

    def owner(frame):
        return ((frame // n_gx) * group + low, lax.rem(frame, n_gx))

    above = (lax.rem(gy + n_gy - 1, n_gy), gx)
    below = (lax.rem(gy + 1, n_gy), gx)
    before = (gy, lax.rem(gx + n_gx - 1, n_gx))
    after = (gy, lax.rem(gx + 1, n_gx))
    me = gy * n_gx + gx
    base = gy - low

    def device(other):
        return (other // n_gx, lax.rem(other, n_gx))

    barrier = pltpu.get_barrier_semaphore()

    def greet(k, carry):
        pl.semaphore_signal(
            barrier, inc=1, device_id=device(lax.rem(me + k, devices)), device_id_type=MESH
        )
        return carry

    lax.fori_loop(1, devices, greet, 0)
    band_ref[...] = band(sw_ref[...], PATCH)
    bias = jnp.concatenate([sb_ref[...].reshape(1, -1)] * PATCH, axis=-1)
    pl.semaphore_wait(barrier, devices - 1)

    def side_copy(k, src, dst, side):
        return pltpu.make_async_remote_copy(
            src_ref=src, dst_ref=dst, send_sem=side_send.at[k], recv_sem=side_recv.at[k],
            device_id=side, device_id_type=MESH,
        )

    vertical = [
        side_copy(0, tall_ref.at[rows - 1], row_in.at[0], below),
        side_copy(1, tall_ref.at[0], row_in.at[1], above),
    ]
    for one in vertical:
        one.start()
    ext[1 : rows + 1] = tall_ref[...]
    for one in vertical:
        one.wait()
    ext[0] = jnp.where(gy > 0, row_in[0], jnp.zeros_like(row_in[0]))
    ext[rows + 1] = jnp.where(gy < n_gy - 1, row_in[1], jnp.zeros_like(row_in[1]))
    edge_out[0] = jnp.concatenate([ext[r, :, lanes - 3 :] for r in range(rows + 2)], axis=-1)
    edge_out[1] = jnp.concatenate([ext[r, :, :3] for r in range(rows + 2)], axis=-1)
    level = [
        side_copy(2, edge_out.at[0], edge_in.at[0], after),
        side_copy(3, edge_out.at[1], edge_in.at[1], before),
    ]
    for one in level:
        one.start()
    loads = [
        pltpu.make_async_copy(src, dst, load_sem.at[k + 1])
        for k, (src, dst) in enumerate(
            ((qkv_hbm, w_ref), (ow_hbm, ow), (wi_hbm, wi), (wo_hbm, wo), (hw_hbm, hw))
        )
    ]

    def edge(k, inside):
        got = edge_in[k]
        got = jnp.where(inside, got, jnp.zeros_like(got))
        return jnp.stack([got[:, 3 * r : 3 * r + 3] for r in range(rows + 2)], axis=0)

    order = list(range(1, patch_cols - 1)) + [0, patch_cols - 1]
    for part in range(parts):
        for spot in range(part_cols):
            col = order[part * part_cols + spot]
            if col == 0:
                for one in level:
                    one.wait()
                cut = jnp.concatenate([edge(0, gx > 0), ext[:, :, : reach - 3]], axis=-1)
            elif col == patch_cols - 1:
                cut = jnp.concatenate(
                    [ext[:, :, lanes - reach + 3 :], edge(1, gx < n_gx - 1)], axis=-1
                )
            else:
                at = 3 * PATCH * col - 3
                cut = ext[:, :, at : at + reach]
            taps = jnp.concatenate([cut[off : off + rows] for off in range(3)], axis=-1)
            for i in range(patch_rows):
                piece = taps[i * PATCH : (i + 1) * PATCH].reshape(PATCH * frames, 3 * reach)
                conv = jnp.dot(piece, band_ref[...], preferred_element_type=F32)
                stem[:, spot, i] = (
                    gelu(conv + bias).astype(BF16).reshape(PATCH, frames, feats)
                )
        if part == 0:
            pw_load.wait()
            for load in loads:
                load.start()
        acc[...] = jnp.zeros_like(acc)

        def step(p, carry):
            acc[...] += jnp.dot(
                stem[p].reshape(part_count, feats),
                pw[pl.ds(pl.multiple_of(p * feats, 64), feats), :],
                preferred_element_type=F32,
            )
            return carry

        lax.fori_loop(0, PATCH, step, 0)
        pieces = []
        for spot in range(part_cols):
            col = order[part * part_cols + spot]
            for i in range(patch_rows):
                at = (spot * patch_rows + i) * frames
                place = pos_ref[i, col : col + 1, :].astype(F32)
                pieces.append((acc[at : at + frames, :] + place).astype(BF16))
        to = lax.broadcasted_iota(jnp.int32, (part_count, part_count), 0)
        fro = lax.broadcasted_iota(jnp.int32, (part_count, part_count), 1)
        swap = jnp.where((to % tiles) * frames + to // tiles == fro, 1.0, 0.0).astype(BF16)
        made[part] = (
            jnp.dot(swap, jnp.concatenate(pieces, axis=0), preferred_element_type=F32)
            .astype(BF16)
            .reshape(frames, tiles, width)
        )

        def start(k, carry):
            to = lax.rem(slot + k, frames)
            pltpu.make_async_remote_copy(
                src_ref=made.at[part, to], dst_ref=got.at[slot, part],
                send_sem=send_sem.at[part, k], recv_sem=recv_sem.at[part, k],
                device_id=owner(to), device_id_type=MESH,
            ).start()
            return carry

        lax.fori_loop(1, frames, start, 0)
        got[slot, part] = made[part, slot]

    count = parts * part_count

    def sequence(part):
        return got[:, part].reshape(part_count, width)

    def kv_copy(k, which, part, place):
        rows = pl.ds(part * part_count, part_count)
        return pltpu.make_async_remote_copy(
            src_ref=kv_ref.at[place, which, rows], dst_ref=kv_ref.at[place, which, rows],
            send_sem=kv_send.at[which, part, k], recv_sem=kv_recv.at[which, part, k],
            device_id=(base + lax.rem(low + k, group), gx), device_id_type=MESH,
        )

    def kv_start(which, part):
        def start(k, carry):
            kv_copy(k, which, part, low).start()
            return carry

        lax.fori_loop(1, group, start, 0)

    def kv_finish(which, part):
        def finish(k, carry):
            kv_copy(k, which, part, lax.rem(low - k + group, group)).wait()
            return carry

        lax.fori_loop(1, group, finish, 0)

    q_gain = qg_ref[...].reshape(1, width)
    k_gain = kg_ref[...].reshape(1, width)

    def project(normed, block, part):
        rows = slice(part * part_count, (part + 1) * part_count)
        for at in range(0, width, 2 * pair):
            both = jnp.dot(
                normed,
                w_ref[:, block * width + at : block * width + at + 2 * pair],
                preferred_element_type=F32,
            )
            for half in range(2):
                tile = both[:, half * pair : (half + 1) * pair]
                lanes = slice(at + half * pair, at + half * pair + pair)
                if block == 0:
                    scaled = head_scale(tile, q_gain[:, lanes]) * HEAD_DIM ** (-0.5)
                    q_ref[rows, lanes] = scaled.astype(BF16)
                elif block == 1:
                    kv_ref[low, 0, rows, lanes] = head_scale(tile, k_gain[:, lanes]).astype(BF16)
                else:
                    kv_ref[low, 1, rows, lanes] = tile.astype(BF16)

    loads[0].wait()
    for part in range(parts):

        def finish(k, carry):
            fro = lax.rem(slot - k + frames, frames)
            pltpu.make_async_remote_copy(
                src_ref=made.at[part, fro], dst_ref=got.at[fro, part],
                send_sem=send_sem.at[part, k], recv_sem=recv_sem.at[part, k],
                device_id=owner(fro), device_id_type=MESH,
            ).wait()
            return carry

        lax.fori_loop(1, frames, finish, 0)
        normed = layer_norm(
            sequence(part).astype(F32), norm_ref[...].reshape(1, width)
        ).astype(BF16)
        project(normed, 2, part)
        kv_start(1, part)
        project(normed, 1, part)
        kv_start(0, part)
        project(normed, 0, part)
    for part in range(parts):
        kv_finish(1, part)
        kv_finish(0, part)

    def attend(lanes, rows):
        q = q_ref[rows, lanes]
        left = lax.broadcasted_iota(jnp.int32, q.shape, 1) < HEAD_DIM
        halves = []
        for side in range(2):
            mine = jnp.where(left if side == 0 else jnp.logical_not(left), q, jnp.zeros_like(q))
            scores = [
                lax.dot_general(
                    mine, kv_ref[g, 0, :, lanes], (((1,), (1,)), ((), ())),
                    preferred_element_type=F32,
                )
                for g in range(group)
            ]
            top = functools.reduce(
                jnp.maximum, [jnp.max(part, -1, keepdims=True) for part in scores]
            )
            totals, mixed = 0.0, 0.0
            for g in range(group):
                expd = jnp.exp(scores[g] - top)
                totals = totals + jnp.sum(expd, -1, keepdims=True)
                mixed = mixed + jnp.dot(
                    expd.astype(BF16), kv_ref[g, 1, :, lanes], preferred_element_type=F32
                )
            halves.append(mixed / totals)
        attended[rows, lanes] = jnp.where(left, halves[0], halves[1]).astype(BF16)

    depth = max(32, 512 // group)

    def each(step, carry):
        at = pl.multiple_of((step // (count // depth)) * pair, pair)
        first = pl.multiple_of(lax.rem(step, count // depth) * depth, depth)
        attend(pl.ds(at, pair), pl.ds(first, depth))
        return carry

    lax.fori_loop(0, (width // pair) * (count // depth), each, 0)

    for load in loads[1:]:
        load.wait()
    total = jnp.zeros((1, width), F32)
    for part in range(parts):
        rows = slice(part * part_count, (part + 1) * part_count)
        stream = sequence(part).astype(F32) + jnp.dot(
            attended[rows, :], ow[...], preferred_element_type=F32
        )
        normed2 = layer_norm(stream, norm2_ref[...].reshape(1, width)).astype(BF16)
        final = stream
        for at in range(0, hidden, width):
            inner = gelu(
                jnp.dot(normed2, wi[:, at : at + width], preferred_element_type=F32)
            ).astype(BF16)
            final = final + jnp.dot(inner, wo[at : at + width, :], preferred_element_type=F32)
        total = total + jnp.sum(
            layer_norm(final, last_ref[...].reshape(1, width)), 0, keepdims=True
        )
    sums[me] = total

    def sum_copy(k, slot):
        return pltpu.make_async_remote_copy(
            src_ref=sums.at[slot], dst_ref=sums.at[slot],
            send_sem=sum_send.at[k], recv_sem=sum_recv.at[k],
            device_id=device(lax.rem(me + k, devices)), device_id_type=MESH,
        )

    def start(k, carry):
        sum_copy(k, me).start()
        return carry

    def finish(k, carry):
        sum_copy(k, lax.rem(me - k + devices, devices)).wait()
        return carry

    lax.fori_loop(1, devices, start, 0)
    lax.fori_loop(1, devices, finish, 0)

    pieces = []
    for frame in range(frames):
        added = 0.0
        for other in range(group):
            added = added + sums[((frame // n_gx) * group + other) * n_gx + frame % n_gx]
        pieces.append(added)
    rest = jnp.concatenate(pieces, axis=0) / (count * group)
    q = 0.0
    for _ in range(3):
        piece = rest.astype(BF16)
        rest = rest - piece.astype(F32)
        q = q + jnp.dot(piece, hw[...], preferred_element_type=F32)
    q = q + b_ref[...].reshape(1, actions)
    out_ref[...] = q
    columns = lax.broadcasted_iota(jnp.int32, (frames, actions), 1)
    same = lax.broadcasted_iota(jnp.int32, (frames, frames), 0) == lax.broadcasted_iota(
        jnp.int32, (frames, frames), 1
    )

    def upright(row):
        return jnp.sum(jnp.where(same, row.astype(F32).reshape(1, frames), 0.0), -1, keepdims=True)

    def pick(index):
        return jnp.sum(jnp.where(index == columns, q, 0.0), -1, keepdims=True)

    chosen = pick(upright(act_ref[...]).astype(jnp.int32))
    picked = [pick(samp_ref[:, s : s + 1]) for s in range(samp_ref.shape[1])]
    top = functools.reduce(jnp.maximum, picked)
    spread = top + jnp.log(sum(jnp.exp(one - top) for one in picked))
    loss = penalty_weight * (spread - chosen) + 0.5 * (chosen - upright(targ_ref[...])) ** 2
    loss_ref[...] = jnp.sum(jnp.where(same, loss, 0.0), 0, keepdims=True)
    mean_ref[...] = jnp.mean(loss, 0, keepdims=True)


def shards(
    images, position, stem_w, stem_b, patch_w, norm_one, qkv_w, q_gain, k_gain, out_w, norm_two,
    mlp_in, mlp_out, norm_last, head_w, head_b, dataset_action, sampled, targets,
):
    n_gy, n_gx = lax.axis_size("gy"), lax.axis_size("gx")
    devices = n_gy * n_gx
    group = devices // images.shape[0]
    assert group * images.shape[0] == devices and n_gy % group == 0
    tall = jnp.transpose(images, (1, 0, 2))
    rows, frames, lanes = tall.shape
    patch_rows, patch_cols, width = position.shape
    feats = PATCH * stem_w.shape[1]
    parts = max(1, patch_rows * patch_cols // 16)
    tiles = patch_rows * patch_cols // parts
    edges = 3 * (rows + 2)
    count = frames * tiles * parts
    dma = pltpu.SemaphoreType.DMA
    q, losses, mean = pl.pallas_call(
        functools.partial(whole_kernel, n_gy, n_gx, group),
        out_shape=(
            jax.ShapeDtypeStruct((frames, head_w.shape[1]), F32),
            jax.ShapeDtypeStruct((1, frames), F32),
            jax.ShapeDtypeStruct((1, 1), F32),
        ),
        in_specs=[vmem()] * 13 + [pl.BlockSpec(memory_space=pl.ANY)] * 6,
        out_specs=(vmem(),) * 3,
        scratch_shapes=[
            pltpu.VMEM((rows + 2, frames, lanes), BF16),
            pltpu.VMEM((2, frames, lanes), BF16),
            pltpu.VMEM((2, frames, edges), BF16),
            pltpu.VMEM((2, frames, edges), BF16),
            pltpu.VMEM((9 * (PATCH + 2), feats), BF16),
            pltpu.VMEM((PATCH, patch_cols // parts, patch_rows, frames, feats), BF16),
            pltpu.VMEM(patch_w.shape, BF16),
            pltpu.VMEM((tiles * frames, width), F32),
            pltpu.VMEM((parts, frames, tiles, width), BF16),
            pltpu.VMEM((frames, parts, tiles, width), BF16),
            pltpu.VMEM((count, width), BF16),
            pltpu.VMEM((group, 2, count, width), BF16),
            pltpu.VMEM((count, width), BF16),
            pltpu.VMEM(qkv_w.shape, BF16),
            pltpu.VMEM(out_w.shape, BF16),
            pltpu.VMEM(mlp_in.shape, BF16),
            pltpu.VMEM(mlp_out.shape, BF16),
            pltpu.VMEM(head_w.shape, BF16),
            pltpu.VMEM((devices, 1, width), F32),
            dma((6,)),
            dma((4,)),
            dma((4,)),
            dma((parts, frames)),
            dma((parts, frames)),
            dma((2, parts, group)),
            dma((2, parts, group)),
            dma((devices,)),
            dma((devices,)),
        ],
        compiler_params=pltpu.CompilerParams(
            collective_id=0, has_side_effects=True, vmem_limit_bytes=VMEM_LIMIT
        ),
        name="whole",
    )(
        tall, position, stem_w, stem_b, norm_one, q_gain, k_gain, norm_two, norm_last, head_b,
        dataset_action, sampled, targets, patch_w, qkv_w, out_w, mlp_in, mlp_out, head_w,
    )
    return q, losses.reshape(frames), mean.reshape(())


def solution(mesh):
    in_specs = (P(None, "gy", "gx"), P("gy", "gx", None)) + (P(),) * 17
    return jax.shard_map(
        shards, mesh=mesh, in_specs=in_specs, out_specs=(P(), P(), P()), check_vma=False
    )
```

time: 87.6 us -> 77.7 us (0.89)
  Pallas kernels: 75.1 us -> 70.5 us
  local copies, waits for them, and re-layouts: 6.86 us -> 4.59 us
  other arithmetic: 1.75 us -> 0 us
  matrix products: 1.13 us -> 0 us
    pallas_call x2 -> x1, Pallas kernels: 75.1 us -> 70.5 us  [shards(): pl.pallas_call(functools.partial(whole_kernel, n_gy, n_gx, group), out_sh...]
    another operation x4 -> x0, local copies, waits for them, and re-layouts: 2.16 us -> none  [the longest x2 1.31 us: own_frames(): jnp.tile(stem_b, PATCH)[None, :]]
    convert_element_type x1 -> x0, other arithmetic: 1.75 us -> none  [band(): return total.astype(BF16)]
    dot_general x1 -> x0, matrix products: 1.13 us -> none  [band(): jnp.dot(jnp.asarray(picks.reshape(-1, 27), BF16), wide, preferred_element...]
where the time goes in v2:
time: 77.7 us; the launch traced here: 77.5 us
  Pallas kernels  70.5 us (91%)
  local copies, waits for them, and re-layouts  4.59 us (6%)
  between operations  2.4 us (3%)
    pallas_call x1, Pallas kernels, shards(): pl.pallas_call(functools.partial(whole_kernel, n_gy, n_gx, group), out_sh...  70.5 us
    unnamed x3, local copies, waits for them, and re-layouts  4.59 us

profile of v2, /device:TPU:0, one launch (start us, length us, event | category | flops | bytes accessed | tf_op | source)
XLA Modules:
  0.0 77.5 jit_solution(1293133132343820585)
XLA Ops:
  0.6 2.0 %copy.24 = bf16[16,56,336]{2,0,1:T(8,128)(2,1)} copy(bf16[16,56,336]{2,1,0:T(8,128)(2,1)} %param.19) | data formatting | bytes 1204224 | tf_op args[0]
  2.7 70.5 %whole.1 = (f32[16,1024]{1,0:T(8,128)}, f32[1,16]{1,0:T(1,128)}, f32[1,1]{1,0:T(1,128)}) custom-call(bf16[56,16,336]{2,1,0:T(8,128)(2,1)} %bitcast.5, bf16[4,8,768]{2,1,0:T(8,128)(2,1)} %pos_ref.1, bf16[27,32]{1,0:T(8,128)(2,1)} %sw_ref.1, f32[32]{0:T(128)} %sb_ref.1, f32[768]{0:T(1024)} %norm_ref.1, f32[768]{0:T(1024)} %qg_ref.1, f32[768]{0:T(1024)} %kg_ref.1, ...), custom_call_target="tpu_custom_call" | custom-call | tf_op jit(solution)/shard_map/whole/pallas_call | solution.py:417
  73.1 1.5 %copy.28 = f32[16,1024]{1,0:T(8,128)} copy(f32[16,1024]{1,0:T(8,128)} %get-tuple-element.12) | data formatting | bytes 131072
  74.6 1.1 %copy.29 = f32[16]{0:T(128)} copy(f32[16]{0:T(128)} %bitcast.6) | data formatting | bytes 128
